TPU v7x, 32 devices: a whole 2x2x4 slice. The times are simulated.
32 devices in a mesh: segment: 2 (over core), tensor: 8 (over z, x), dp: 2 (over y).
Axes of the slice: x: 2, y: 2, z: 4, core: 2. Of those that a mesh axis runs over, the one named last changes fastest.
Arguments:
- tokens: bfloat16 [256, 1536], P('dp', 'tensor'), may hold values from -6 to 6
- w_gate: bfloat16 [2, 1536, 12288], P('segment', None, 'tensor'), may hold values from -0.15625 to 0.15625
- w_up: bfloat16 [2, 1536, 12288], P('segment', None, 'tensor'), may hold values from -0.15625 to 0.15625
- w_down: bfloat16 [2, 12288, 1536], P('segment', 'tensor'), may hold values from -0.0546875 to 0.0546875
- cotangent: bfloat16 [256, 1536], P('dp', 'tensor'), may hold values from -0.1796875 to 0.1796875
Outputs:
- grad_gate: float32 [2, 1536, 12288], P('segment', 'dp', 'tensor')
- grad_up: float32 [2, 1536, 12288], P('segment', 'dp', 'tensor')
- grad_down: float32 [2, 12288, 1536], P('segment', 'tensor', 'dp')
All inputs are finite; a program needn't handle non-finite values.
Results may differ from a plain program's by a relative error of at most 0.023.
Values may be sent and summed in bfloat16 or wider, within the bound.
A program may use at most 64 MiB of HBM per device.

v0:
```python
import jax
import jax.numpy as jnp
from jax import lax
from jax.sharding import PartitionSpec as P

MICRO = 2


def from_behind(block, axis, distance):
    devices = range(lax.axis_size(axis))
    route = [(i - distance, i) for i in devices if i - distance in devices]
    return lax.ppermute(block, axis, route)


def shortened(value):

    def short(part):
        return part.astype(jnp.bfloat16) if part.dtype == jnp.float32 else part

    return jax.tree.map(short, value)


def select_tick(stored, position):
    if 0 <= position < len(stored):
        return stored[position]
    return jnp.zeros_like(stored[0])


def against_cols(left, right):
    return lax.dot_general(
        left, right, (((1,), (1,)), ((), ())), preferred_element_type=jnp.float32
    )


def replica_rounded(left, right, replicas):
    left_blocks = left.reshape(replicas, -1, left.shape[1])
    right_blocks = right.reshape(replicas, -1, right.shape[1])
    terms = jnp.einsum(
        "rtd,rtf->rdf", left_blocks, right_blocks, preferred_element_type=jnp.float32
    )
    terms = lax.optimization_barrier(terms.astype(jnp.bfloat16)).astype(jnp.float32)
    return jnp.sum(terms, axis=0)


def local(tokens, w_gate, w_up, w_down, cotangent):
    gate_weight = w_gate[0]
    up_weight = w_up[0]
    down_weight = w_down[0]
    leading = lax.axis_index("segment") == 0
    row_count = tokens.shape[0] // MICRO
    hidden_cols = gate_weight.shape[1]
    blank_rows = jnp.zeros((row_count, tokens.shape[1]), jnp.bfloat16)
    blank_hidden = jnp.zeros((row_count, hidden_cols), jnp.bfloat16)
    received = blank_rows
    gathers = []
    gates = []
    ups = []
    evicted = []
    for moment in range(MICRO + 1):
        fresh_rows = (
            tokens[moment * row_count : (moment + 1) * row_count] if moment < MICRO else blank_rows
        )
        inputs = jnp.where(leading, fresh_rows, received)
        gathered = lax.all_gather(inputs, "tensor", axis=1, tiled=True)
        gate_store = jnp.dot(gathered, gate_weight, preferred_element_type=jnp.float32).astype(
            jnp.bfloat16
        )
        up_store = jnp.dot(gathered, up_weight, preferred_element_type=jnp.float32).astype(
            jnp.bfloat16
        )
        hidden = (
            jax.nn.silu(gate_store.astype(jnp.float32)) * up_store.astype(jnp.float32)
        ).astype(jnp.bfloat16)
        partial_value = jnp.dot(hidden, down_weight, preferred_element_type=jnp.float32)
        mixed_sum = lax.psum_scatter(
            partial_value.astype(jnp.bfloat16), "tensor", scatter_dimension=1, tiled=True
        ).astype(jnp.float32)
        output = (inputs.astype(jnp.float32) + mixed_sum).astype(jnp.bfloat16)
        gathers.append(gathered)
        gates.append(gate_store)
        ups.append(up_store)
        if moment < MICRO:
            received = from_behind(output, "segment", 1)
            evicted.append(from_behind((gate_store, up_store), "segment", 1))
    received_back = blank_rows
    records = []
    for moment in range(MICRO + 1):
        fresh_rows = (
            cotangent[moment * row_count : (moment + 1) * row_count]
            if moment < MICRO
            else blank_rows
        )
        upstream = jnp.where(leading, received_back, fresh_rows)
        gathered = jnp.where(
            leading, select_tick(gathers, moment - 1), select_tick(gathers, moment + 1)
        )
        if moment >= 1:
            gate_back, up_back = from_behind(shortened(evicted[moment - 1]), "segment", -1)
        else:
            gate_back, up_back = (blank_hidden, blank_hidden)
        gate_store = jnp.where(leading, gate_back, select_tick(gates, moment + 1))
        up_store = jnp.where(leading, up_back, select_tick(ups, moment + 1))
        gate_value = gate_store.astype(jnp.float32)
        up_value = up_store.astype(jnp.float32)
        hidden = (jax.nn.silu(gate_value) * up_value).astype(jnp.bfloat16)
        cot_full = lax.all_gather(upstream, "tensor", axis=1, tiled=True)
        d_hidden = against_cols(cot_full, down_weight)
        sigma = jax.nn.sigmoid(gate_value)
        d_gate = (d_hidden * up_value * sigma * (1.0 + gate_value * (1.0 - sigma))).astype(
            jnp.bfloat16
        )
        d_up = (d_hidden * gate_value * sigma).astype(jnp.bfloat16)
        records.append((gathered, d_gate, d_up, cot_full, hidden))
        if moment < MICRO:
            partial_value = against_cols(d_gate, gate_weight) + against_cols(d_up, up_weight)
            summed = lax.psum_scatter(
                partial_value.astype(jnp.bfloat16), "tensor", scatter_dimension=1, tiled=True
            ).astype(jnp.float32)
            d_input = (upstream.astype(jnp.float32) + summed).astype(jnp.bfloat16)
            received_back = from_behind(d_input, "segment", -1)
    all_gathered = jnp.concatenate([entry[0] for entry in records], axis=0)
    all_gate = jnp.concatenate([entry[1] for entry in records], axis=0)
    all_up = jnp.concatenate([entry[2] for entry in records], axis=0)
    all_cot = jnp.concatenate([entry[3] for entry in records], axis=0)
    all_hidden = jnp.concatenate([entry[4] for entry in records], axis=0)
    replicas = lax.axis_size("dp")
    feature_cols, cot_cols = (
        lax.all_to_all(all_gathered, "dp", split_axis=1, concat_axis=0, tiled=True),
        lax.all_to_all(all_cot, "dp", split_axis=1, concat_axis=0, tiled=True),
    )
    every_gate, every_up, every_hidden = (
        lax.all_gather(all_gate, "dp", axis=0, tiled=True),
        lax.all_gather(all_up, "dp", axis=0, tiled=True),
        lax.all_gather(all_hidden, "dp", axis=0, tiled=True),
    )
    reduced = jnp.concatenate(
        [
            replica_rounded(feature_cols, every_gate, replicas),
            replica_rounded(feature_cols, every_up, replicas),
            replica_rounded(cot_cols, every_hidden, replicas),
        ],
        axis=1,
    )
    grad_gate = reduced[:, :hidden_cols][None]
    grad_up = reduced[:, hidden_cols : 2 * hidden_cols][None]
    grad_down = reduced[:, 2 * hidden_cols :].T[None]
    return (grad_gate, grad_up, grad_down)


def solution(mesh):
    in_specs = (
        P("dp", "tensor"),
        P("segment", None, "tensor"),
        P("segment", None, "tensor"),
        P("segment", "tensor", None),
        P("dp", "tensor"),
    )
    out_specs = (
        P("segment", "dp", "tensor"),
        P("segment", "dp", "tensor"),
        P("segment", "tensor", "dp"),
    )
    return jax.shard_map(local, mesh=mesh, in_specs=in_specs, out_specs=out_specs, check_vma=False)
```

profile of v0, /device:TPU:0, one launch (start us, length us, event | category | flops | bytes accessed | tf_op | source)
XLA Modules:
  0.0 585.2 jit_solution(2344201847829051952)
XLA Ops:
  7.2 1.0 fusion.120
  8.3 32.5 %all-gather = bf16[8,192,64]{1,2,0:T(8,128)(2,1)S(1)} all-gather(bf16[1,192,64]{1,2,0:T(8,128)(2,1)S(1)} %fusion.113), channel_id=1, replica_groups=mesh['segment'=2,'tensor'=8,'dp'=2] {'tensor'}, dimensions={0}, use_global_device_ids=true | all-gather | bytes 221184 | tf_op jit(solution)/shard_map/all_gather | solution.py:64
  41.2 3.4 fusion.42
  44.7 2.1 collective-permute-start.5
  46.8 0.9 fusion.51
  47.7 2.0 collective-permute-start.3
  49.7 0.9 fusion.60
  50.6 0.9 copy.37
  51.8 62.3 %reduce-scatter.13.cloned.1.call-done = bf16[192,64]{1,0:T(8,128)(2,1)} async-done(((bf16[1536,64]{1,0:T(8,128)(2,1)}), bf16[192,64]{1,0:T(8,128)(2,1)}) %reduce-scatter.13.cloned.1.call-update) | async-done | bytes 24592
  114.1 0.9 copy.38
  115.1 1.3 collective-permute-start
  116.4 30.9 %all-gather.3 = bf16[8,192,64]{1,2,0:T(8,128)(2,1)S(1)} all-gather(bf16[1,192,64]{1,2,0:T(8,128)(2,1)S(1)} %fusion.114), channel_id=1, replica_groups=mesh['segment'=2,'tensor'=8,'dp'=2] {'tensor'}, dimensions={0}, use_global_device_ids=true | all-gather | bytes 221184 | tf_op jit(solution)/shard_map/all_gather | solution.py:106
  147.8 30.8 %all-gather.1 = bf16[8,192,64]{1,2,0:T(8,128)(2,1)S(1)} all-gather(bf16[1,192,64]{1,2,0:T(8,128)(2,1)S(1)} %fusion.115), channel_id=1, replica_groups=mesh['segment'=2,'tensor'=8,'dp'=2] {'tensor'}, dimensions={0}, use_global_device_ids=true | all-gather | bytes 221184 | tf_op jit(solution)/shard_map/all_gather | solution.py:64
  179.0 3.4 fusion.54
  182.4 3.3 fusion.45
  185.7 0.9 fusion.63
  186.6 0.9 copy.39
  187.6 3.9 fusion.79
  191.5 3.9 fusion.14
  195.4 3.9 fusion.39
  199.3 0.9 copy.41
  200.4 1.3 collective-permute-start.6
  201.7 1.3 collective-permute-start.4
  203.0 45.3 %reduce-scatter.15.cloned.1.call-done = bf16[192,64]{1,0:T(8,128)(2,1)} async-done(((bf16[1536,64]{1,0:T(8,128)(2,1)}), bf16[192,64]{1,0:T(8,128)(2,1)}) %reduce-scatter.15.cloned.1.call-update) | async-done | bytes 24592
  248.3 0.9 copy.40
  249.2 1.3 collective-permute-start.1
  250.5 62.1 %reduce-scatter.17.cloned.1.call-done = bf16[192,64]{1,0:T(8,128)(2,1)} async-done(((bf16[1536,64]{1,0:T(8,128)(2,1)}), bf16[192,64]{1,0:T(8,128)(2,1)}) %reduce-scatter.17.cloned.1.call-update) | async-done | bytes 24592
  312.6 0.9 copy.42
  313.5 1.3 collective-permute-start.2
  314.8 30.9 %all-gather.2 = bf16[8,192,64]{1,2,0:T(8,128)(2,1)S(1)} all-gather(bf16[1,192,64]{1,2,0:T(8,128)(2,1)S(1)} %select_bitcast_fusion.4), channel_id=1, replica_groups=mesh['segment'=2,'tensor'=8,'dp'=2] {'tensor'}, dimensions={0}, use_global_device_ids=true | all-gather | bytes 221184 | tf_op jit(solution)/shard_map/all_gather | solution.py:64
  346.1 3.3 fusion.57
  349.4 30.9 %all-gather.4 = bf16[8,192,64]{1,2,0:T(8,128)(2,1)S(1)} all-gather(bf16[1,192,64]{1,2,0:T(8,128)(2,1)S(1)} %fusion.116), channel_id=1, replica_groups=mesh['segment'=2,'tensor'=8,'dp'=2] {'tensor'}, dimensions={0}, use_global_device_ids=true | all-gather | bytes 221184 | tf_op jit(solution)/shard_map/all_gather | solution.py:106
  380.8 4.0 fusion.2
  384.8 3.3 fusion.48
  388.7 1.5 fusion.10
  390.2 1.5 fusion.36
  391.8 0.9 copy.43
  392.8 1.3 collective-permute-start.10
  394.1 1.3 collective-permute-start.8
  395.4 58.0 %reduce-scatter.19.cloned.1.call-done = bf16[192,64]{1,0:T(8,128)(2,1)} async-done(((bf16[1536,64]{1,0:T(8,128)(2,1)}), bf16[192,64]{1,0:T(8,128)(2,1)}) %reduce-scatter.19.cloned.1.call-update) | async-done | bytes 24592
  453.4 0.9 copy.44
  454.3 1.3 collective-permute-start.7
  455.6 1.3 collective-permute-start.11
  456.9 1.3 collective-permute-start.9
  458.2 30.9 %all-gather.5 = bf16[8,192,64]{1,2,0:T(8,128)(2,1)S(1)} all-gather(bf16[1,192,64]{1,2,0:T(8,128)(2,1)S(1)} %select_bitcast_fusion.3), channel_id=1, replica_groups=mesh['segment'=2,'tensor'=8,'dp'=2] {'tensor'}, dimensions={0}, use_global_device_ids=true | all-gather | bytes 221184 | tf_op jit(solution)/shard_map/all_gather | solution.py:106
  489.5 3.9 fusion.106
  493.4 0.9 pad_maximum_fusion.4
  494.4 0.9 pad_maximum_fusion.1
  495.3 0.9 copy.53
  496.2 3.5 all-to-all-start.1
  499.8 0.9 copy.54
  500.7 0.8 pad_maximum_fusion.2
  501.5 13.0 %all-to-all-done.1 = bf16[192,2,768]{2,0,1:T(8,128)(2,1)S(1)} async-done(((bf16[192,2,768]{2,0,1:T(8,128)(2,1)}), bf16[192,2,768]{2,0,1:T(8,128)(2,1)S(1)}, u32[]{:S(2)}, u32[]{:S(2)}) %all-to-all-start.1) | async-done | bytes 589856 | tf_op jit(solution)/shard_map/all_to_all | solution.py:129
  514.5 3.7 all-to-all-start
  518.2 4.6 all-gather.14.cloned.1.call-done
  522.9 2.7 convolution_convert_fusion
  525.6 3.1 convert_reduce_fusion
  528.7 6.1 %copy.36 = f32[1,1536,768]{2,1,0:T(8,128)} copy(f32[1,1536,768]{1,2,0:T(8,128)} %bitcast.160) | data formatting | bytes 9437184
  534.8 13.4 %all-gather.10.cloned.1.call-done = bf16[384,1536]{1,0:T(8,128)(2,1)} async-done(((bf16[192,1536]{1,0:T(8,128)(2,1)}), bf16[384,1536]{1,0:T(8,128)(2,1)}) %all-gather.10.cloned.1.call-update) | async-done | bytes 1179664 | tf_op jit(solution)/shard_map/all_gather | solution.py:132
  548.2 2.7 convolution_convert_fusion.2
  550.9 3.1 convert_reduce_fusion.2
  554.0 18.6 %all-gather.12.cloned.1.call-done = bf16[384,1536]{1,0:T(8,128)(2,1)} async-done(((bf16[192,1536]{1,0:T(8,128)(2,1)}), bf16[384,1536]{1,0:T(8,128)(2,1)}) %all-gather.12.cloned.1.call-update) | async-done | bytes 1179664 | tf_op jit(solution)/shard_map/all_gather | solution.py:133
  572.5 2.7 convolution_convert_fusion.1
  575.3 3.1 convert_reduce_fusion.1
  (81 shorter events, 3.9 us)
Async XLA Ops:
  7.2 107.0 %reduce-scatter.13.cloned.1.call-start = ((), (), s32[]{:S(2)}) async-start(), calls=%async_computation.9 | async-start | bytes 442368
  41.2 5.6 copy-start
  41.2 8.5 %copy-start.1 = (bf16[1,1536,1536]{2,1,0:T(8,128)(2,1)S(1)}, bf16[1,1536,1536]{2,1,0:T(8,128)(2,1)}, u32[]{:S(2)}) copy-start(bf16[1,1536,1536]{2,1,0:T(8,128)(2,1)} %param.8) | copy-start | bytes 14155780
  44.6 7.0 %copy-start.2 = (bf16[128,192]{0,1:T(8,128)(2,1)S(1)}, bf16[128,192]{0,1:T(8,128)(2,1)}, u32[]{:S(2)}) copy-start(bf16[128,192]{0,1:T(8,128)(2,1)} %param.9) | copy-start | bytes 147460
  44.7 155.7 %collective-permute-start.5 = (bf16[64,1536]{1,0:T(8,128)(2,1)S(1)}, bf16[64,1536]{1,0:T(8,128)(2,1)}, u32[]{:S(2)}, u32[]{:S(2)}) collective-permute-start(bf16[64,1536]{1,0:T(8,128)(2,1)S(1)} %fusion.42), channel_id=1, source_target_pairs={{0,16},{1,17},{2,18},{3,19},{4,20},{5,21},{6,22},{7,23},{8,24},{9,... | collective-permute-start | bytes 589832 | tf_op jit(solution)/shard_map/ppermute | solution.py:12
  47.7 154.0 %collective-permute-start.3 = (bf16[64,1536]{1,0:T(8,128)(2,1)S(1)}, bf16[64,1536]{1,0:T(8,128)(2,1)}, u32[]{:S(2)}, u32[]{:S(2)}) collective-permute-start(bf16[64,1536]{1,0:T(8,128)(2,1)S(1)} %fusion.51), channel_id=1, source_target_pairs={{0,16},{1,17},{2,18},{3,19},{4,20},{5,21},{6,22},{7,23},{8,24},{9,... | collective-permute-start | bytes 589832 | tf_op jit(solution)/shard_map/ppermute | solution.py:12
  51.6 196.7 %reduce-scatter.15.cloned.1.call-start = ((), (), s32[]{:S(2)}) async-start(), calls=%async_computation.10 | async-start | bytes 442368
  115.1 32.7 %collective-permute-start = (bf16[64,192]{1,0:T(8,128)(2,1)S(1)}, bf16[64,192]{1,0:T(8,128)(2,1)S(1)}, u32[]{:S(2)}, u32[]{:S(2)}) collective-permute-start(bf16[64,192]{1,0:T(8,128)(2,1)S(1)} %add_convert_fusion.3), channel_id=1, source_target_pairs={{0,16},{1,17},{2,18},{3,19},{4,20},{5,21},{6,22},{7,23},{8,24},{9,... | collective-permute-start | bytes 73736 | tf_op jit(solution)/shard_map/ppermute | solution.py:12
  178.7 7.0 %slice-start.4 = ((s8[4718592]{0:T(1024)(128)(4,1)}), s8[524288]{0:T(1024)(128)(4,1)S(1)}, s32[]{:S(2)}) async-start(s8[4718592]{0:T(1024)(128)(4,1)} %bitcast.158), calls=%async_computation.17 | async-start | bytes 1048576
  179.0 6.7 %slice-start.5 = ((s8[4718592]{0:T(1024)(128)(4,1)}), s8[4194304]{0:T(1024)(128)(4,1)S(1)}, s32[]{:S(2)}) async-start(s8[4718592]{0:T(1024)(128)(4,1)} %bitcast.158), calls=%async_computation.18 | async-start | bytes 8388608
  187.6 125.0 %reduce-scatter.17.cloned.1.call-start = ((), (), s32[]{:S(2)}) async-start(), calls=%async_computation.11 | async-start | bytes 442368
  200.2 253.1 %reduce-scatter.19.cloned.1.call-start = ((), (), s32[]{:S(2)}) async-start(), calls=%async_computation.12 | async-start | bytes 442368
  200.4 187.8 %collective-permute-start.6 = (bf16[64,1536]{1,0:T(8,128)(2,1)}, bf16[64,1536]{1,0:T(8,128)(2,1)S(1)}, u32[]{:S(2)}, u32[]{:S(2)}) collective-permute-start(bf16[64,1536]{1,0:T(8,128)(2,1)} %collective-permute-done.5), channel_id=1, source_target_pairs={{16,0},{17,1},{18,2},{19,3},{20,4},{21,5},{22,6},{23,7},{24,8},{25... | collective-permute-start | bytes 589832 | tf_op jit(solution)/shard_map/ppermute | solution.py:12
  201.7 186.5 %collective-permute-start.4 = (bf16[64,1536]{1,0:T(8,128)(2,1)}, bf16[64,1536]{1,0:T(8,128)(2,1)S(1)}, u32[]{:S(2)}, u32[]{:S(2)}) collective-permute-start(bf16[64,1536]{1,0:T(8,128)(2,1)} %collective-permute-done.3), channel_id=1, source_target_pairs={{16,0},{17,1},{18,2},{19,3},{20,4},{21,5},{22,6},{23,7},{24,8},{25... | collective-permute-start | bytes 589832 | tf_op jit(solution)/shard_map/ppermute | solution.py:12
  249.2 65.6 %collective-permute-start.1 = (bf16[64,192]{1,0:T(8,128)(2,1)S(1)}, bf16[64,192]{1,0:T(8,128)(2,1)S(1)}, u32[]{:S(2)}, u32[]{:S(2)}) collective-permute-start(bf16[64,192]{1,0:T(8,128)(2,1)S(1)} %add_convert_fusion.2), channel_id=1, source_target_pairs={{0,16},{1,17},{2,18},{3,19},{4,20},{5,21},{6,22},{7,23},{8,24},{9,... | collective-permute-start | bytes 73736 | tf_op jit(solution)/shard_map/ppermute | solution.py:12
  313.5 35.9 %collective-permute-start.2 = (bf16[64,192]{1,0:T(8,128)(2,1)S(1)}, bf16[64,192]{1,0:T(8,128)(2,1)S(1)}, u32[]{:S(2)}, u32[]{:S(2)}) collective-permute-start(bf16[64,192]{1,0:T(8,128)(2,1)S(1)} %add_convert_fusion.1), channel_id=1, source_target_pairs={{16,0},{17,1},{18,2},{19,3},{20,4},{21,5},{22,6},{23,7},{24,8},{25... | collective-permute-start | bytes 73736 | tf_op jit(solution)/shard_map/ppermute | solution.py:12
  380.8 7.9 %slice-start = ((s8[4718592]{0:T(1024)(128)(4,1)}), s8[4194304]{0:T(1024)(128)(4,1)S(1)}, s32[]{:S(2)}) async-start(s8[4718592]{0:T(1024)(128)(4,1)} %bitcast.154), calls=%async_computation.13 | async-start | bytes 8388608
  380.8 9.4 %slice-start.2 = ((s8[4718592]{0:T(1024)(128)(4,1)}), s8[4194304]{0:T(1024)(128)(4,1)S(1)}, s32[]{:S(2)}) async-start(s8[4718592]{0:T(1024)(128)(4,1)} %bitcast.156), calls=%async_computation.15 | async-start | bytes 8388608
  384.8 3.8 slice-start.1
  384.8 5.4 slice-start.3
  392.7 130.2 %all-gather.14.cloned.1.call-start = ((), (), s32[]{:S(2)}) async-start(), calls=%async_computation.8 | async-start | bytes 1769472 | tf_op jit(solution)/shard_map/all_gather | solution.py:134
  392.8 62.8 %collective-permute-start.10 = (bf16[64,1536]{1,0:T(8,128)(2,1)S(1)}, bf16[64,1536]{1,0:T(8,128)(2,1)S(1)}, u32[]{:S(2)}, u32[]{:S(2)}) collective-permute-start(bf16[64,1536]{1,0:T(8,128)(2,1)S(1)} %fusion.45), channel_id=1, source_target_pairs={{0,16},{1,17},{2,18},{3,19},{4,20},{5,21},{6,22},{7,23},{8,24},{9,... | collective-permute-start | bytes 589832 | tf_op jit(solution)/shard_map/ppermute | solution.py:12
  394.1 62.8 %collective-permute-start.8 = (bf16[64,1536]{1,0:T(8,128)(2,1)S(1)}, bf16[64,1536]{1,0:T(8,128)(2,1)S(1)}, u32[]{:S(2)}, u32[]{:S(2)}) collective-permute-start(bf16[64,1536]{1,0:T(8,128)(2,1)S(1)} %fusion.54), channel_id=1, source_target_pairs={{0,16},{1,17},{2,18},{3,19},{4,20},{5,21},{6,22},{7,23},{8,24},{9,... | collective-permute-start | bytes 589832 | tf_op jit(solution)/shard_map/ppermute | solution.py:12
  454.3 3.9 collective-permute-start.7
  455.6 33.9 %collective-permute-start.11 = (bf16[64,1536]{1,0:T(8,128)(2,1)S(1)}, bf16[64,1536]{1,0:T(8,128)(2,1)S(1)}, u32[]{:S(2)}, u32[]{:S(2)}) collective-permute-start(bf16[64,1536]{1,0:T(8,128)(2,1)S(1)} %collective-permute-done.10), channel_id=1, source_target_pairs={{16,0},{17,1},{18,2},{19,3},{20,4},{21,5},{22,6},{23,7},{24,8},{25... | collective-permute-start | bytes 589832 | tf_op jit(solution)/shard_map/ppermute | solution.py:12
  456.9 32.6 %collective-permute-start.9 = (bf16[64,1536]{1,0:T(8,128)(2,1)S(1)}, bf16[64,1536]{1,0:T(8,128)(2,1)}, u32[]{:S(2)}, u32[]{:S(2)}) collective-permute-start(bf16[64,1536]{1,0:T(8,128)(2,1)S(1)} %collective-permute-done.8), channel_id=1, source_target_pairs={{16,0},{17,1},{18,2},{19,3},{20,4},{21,5},{22,6},{23,7},{24,8},{25... | collective-permute-start | bytes 589832 | tf_op jit(solution)/shard_map/ppermute | solution.py:12
  494.3 53.9 %all-gather.10.cloned.1.call-start = ((), (), s32[]{:S(2)}) async-start(), calls=%async_computation.6 | async-start | bytes 1769472 | tf_op jit(solution)/shard_map/all_gather | solution.py:132
  496.2 18.3 %all-to-all-start.1 = ((bf16[192,2,768]{2,0,1:T(8,128)(2,1)}), bf16[192,2,768]{2,0,1:T(8,128)(2,1)S(1)}, u32[]{:S(2)}, u32[]{:S(2)}) async-start(bf16[192,2,768]{2,0,1:T(8,128)(2,1)} %bitcast.152), calls=%async_computation.1 | async-start | bytes 1179648 | tf_op jit(solution)/shard_map/all_to_all | solution.py:129
  499.7 72.8 %all-gather.12.cloned.1.call-start = ((), (), s32[]{:S(2)}) async-start(), calls=%async_computation.7 | async-start | bytes 1769472 | tf_op jit(solution)/shard_map/all_gather | solution.py:133
  514.5 20.3 %all-to-all-start = ((bf16[192,2,768]{2,0,1:T(8,128)(2,1)}), bf16[192,2,768]{2,0,1:T(8,128)(2,1)S(1)}, u32[]{:S(2)}, u32[]{:S(2)}) async-start(bf16[192,2,768]{2,0,1:T(8,128)(2,1)} %bitcast.153), calls=%async_computation | async-start | bytes 1179648 | tf_op jit(solution)/shard_map/all_to_all | solution.py:128
Sparse Core Ops, SparseCore 0:
  51.7 62.3 reduce-scatter.12
  187.7 60.5 reduce-scatter.14
  252.1 60.4 reduce-scatter.16
  392.8 60.4 reduce-scatter.18
  494.4 28.4 all-gather.13
  524.8 23.2 all-gather.9
  549.7 22.7 all-gather.11
where the time goes:
time: 586 us; the launch traced here: 585 us
  waiting for transfers between devices  277 us (47%)
  blocking collectives  187 us (32%)
  matrix products  50.2 us (9%)
  starting transfers between devices  24.5 us (4%)
  local copies, waits for them, and re-layouts  18.7 us (3%)
  between operations  14.8 us (3%)
  other arithmetic  12.5 us (2%)
    unnamed x11, waiting for transfers between devices  228 us
    all_gather x3, blocking collectives, local(): gathered = lax.all_gather(inputs, 'tensor', axis=1, tiled=True)  94.3 us
    all_gather x3, blocking collectives, local(): cot_full = lax.all_gather(upstream, 'tensor', axis=1, tiled=True)  92.7 us
    dot_general x7, matrix products, against_cols(): lax.dot_general(left, right, (((1,), (1,)), ((), ())), preferred_element_...  22.6 us
    all_gather x1, waiting for transfers between devices, local(): lax.all_gather(all_up, 'dp', axis=0, tiled=True)  18.6 us
    ppermute x12, starting transfers between devices, from_behind(): return lax.ppermute(block, axis, route)  17 us
    unnamed x37, local copies, waits for them, and re-layouts  15.1 us
    all_gather x1, waiting for transfers between devices, local(): lax.all_gather(all_gate, 'dp', axis=0, tiled=True)  13.4 us
  transfers between devices with their start and end apart: 21, of which 8 were waited for; matrix products, arithmetic and copies ran while one was open for 11% of the time, Pallas kernels for 0%

commit v1 on v0

v1 whole, which is shorter than its diff:
```python
import functools

import jax
import jax.numpy as jnp
from jax import lax
from jax.experimental import pallas as pl
from jax.experimental.pallas import tpu as pltpu
from jax.sharding import PartitionSpec as P

MESH = pl.DeviceIdType.MESH
VMEM_LIMIT = 56 * 1024 * 1024


def tile_of(size):
    for tile in (512, 256, 128):
        if size % tile == 0:
            return tile
    return size


def dot(left, right):
    return jnp.dot(left, right, preferred_element_type=jnp.float32)


def dot_nt(left, right):
    return lax.dot_general(
        left, right, (((1,), (1,)), ((), ())), preferred_element_type=jnp.float32
    )


def dot_tn(left, right):
    return lax.dot_general(
        left, right, (((0,), (0,)), ((), ())), preferred_element_type=jnp.float32
    )


def hidden_of(gate, up):
    g = gate.astype(jnp.float32)
    return (g * jax.nn.sigmoid(g) * up.astype(jnp.float32)).astype(jnp.bfloat16)


def slopes(gate, up, d_hidden):
    g = gate.astype(jnp.float32)
    u = up.astype(jnp.float32)
    q = jax.nn.sigmoid(g)
    d_gate = (d_hidden * u * q * (1.0 + g * (1.0 - q))).astype(jnp.bfloat16)
    d_up = (d_hidden * g * q).astype(jnp.bfloat16)
    return d_gate, d_up


def relay_kernel(
    n, ndp, block,
    tok, cot, wg_h, wu_h, wd_h,
    a_out, b_out, h_out, dg_out, du_out,
    wg, wu, wd, shards, a_all, b_all, gate_s, up_s, hid, dgate, dup, dhid, stage, sums, turned,
    w_sem, out_sem, ag_send, ag_recv, ax_send, ax_recv, rs_send, rs_recv, bc_send, bc_recv, fw_send, fw_recv,
):
    seg = lax.axis_index("segment")
    t = lax.axis_index("tensor")
    d = lax.axis_index("dp")
    other = 1 - seg
    rows, depth = a_all.shape[1], a_all.shape[2]
    wide = hid.shape[2]
    part = tok.shape[1]
    holders = rows // block
    ff_tile, d_tile = tile_of(wide), tile_of(depth)

    loads = [
        pltpu.make_async_copy(source.at[0], target, w_sem.at[i])
        for i, (source, target) in enumerate(((wg_h, wg), (wu_h, wu), (wd_h, wd)))
    ]
    for load in loads:
        load.start()

    def place(s, x, y):
        return {"segment": s, "tensor": x, "dp": y}

    barrier = pltpu.get_barrier_semaphore()

    @pl.loop(0, n)
    def _(k):
        peer = lax.rem(t + k, n)
        pl.semaphore_signal(barrier, inc=1, device_id=place(other, peer, d), device_id_type=MESH)

        @pl.when(k > 0)
        def _():
            pl.semaphore_signal(barrier, inc=1, device_id=place(seg, peer, d), device_id_type=MESH)

    for r in range(1, ndp):
        pl.semaphore_signal(
            barrier, inc=1, device_id=place(seg, t, lax.rem(d + r, ndp)), device_id_type=MESH
        )
    shards[t] = jnp.where(seg == 0, tok[...], cot[...])
    pl.semaphore_wait(barrier, 2 * n - 1 + ndp - 1)

    def ag_copy(k, slot, peer):
        return pltpu.make_async_remote_copy(
            src_ref=shards.at[slot], dst_ref=shards.at[slot],
            send_sem=ag_send.at[k], recv_sem=ag_recv.at[k],
            device_id=place(seg, peer, d), device_id_type=MESH,
        )

    def ax_copy(r, slot):
        return pltpu.make_async_remote_copy(
            src_ref=a_all.at[slot], dst_ref=a_all.at[slot],
            send_sem=ax_send.at[r], recv_sem=ax_recv.at[r],
            device_id=place(seg, t, lax.rem(d + r, ndp)), device_id_type=MESH,
        )

    def rs_copy(k, owner, slot, peer):
        return pltpu.make_async_remote_copy(
            src_ref=stage.at[pl.ds(pl.multiple_of(owner * block, block), block)],
            dst_ref=sums.at[slot],
            send_sem=rs_send.at[k], recv_sem=rs_recv.at[k],
            device_id=place(seg, peer, d), device_id_type=MESH,
        )

    def bc_copy(k, owner, peer):
        return pltpu.make_async_remote_copy(
            src_ref=turned,
            dst_ref=b_all.at[d, pl.ds(pl.multiple_of(owner * block, block), block)],
            send_sem=bc_send.at[k], recv_sem=bc_recv.at[k],
            device_id=place(other, peer, d), device_id_type=MESH,
        )

    def fw_copy(r, k, slot, owner):
        here = b_all.at[slot, pl.ds(pl.multiple_of(owner * block, block), block)]
        return pltpu.make_async_remote_copy(
            src_ref=here, dst_ref=here,
            send_sem=fw_send.at[r, k], recv_sem=fw_recv.at[r, k],
            device_id=place(seg, t, lax.rem(d + r, ndp)), device_id_type=MESH,
        )

    def if_holder(index, action):
        if holders == n:
            action()
        else:
            pl.when(index < holders)(action)

    @pl.loop(1, n)
    def _(k):
        ag_copy(k, t, lax.rem(t + k, n)).start()

    @pl.loop(1, n)
    def _(k):
        ag_copy(k, lax.rem(t - k + n, n), t).wait_recv()

    for i in range(n):
        a_all[d, :, i * part:(i + 1) * part] = shards[i]
    for r in range(1, ndp):
        ax_copy(r, d).start()
    for load in loads:
        load.wait()

    def reduce_rows():
        @pl.loop(1, n)
        def _(k):
            peer = lax.rem(t + k, n)
            if_holder(peer, lambda: rs_copy(k, peer, t, peer).start())

        def total():
            mine = pl.ds(pl.multiple_of(t * block, block), block)
            sums[t] = stage[mine, :]

            @pl.loop(1, n)
            def _(k):
                rs_copy(k, t, lax.rem(t - k + n, n), t).wait_recv()

            value = sums[0].astype(jnp.float32)
            for i in range(1, n):
                value = value + sums[i].astype(jnp.float32)
            turned[...] = (a_all[d, mine, :].astype(jnp.float32) + value).astype(jnp.bfloat16)

            @pl.loop(0, n)
            def _(k):
                bc_copy(k, t, lax.rem(t + k, n)).start()

        if_holder(t, total)

    def reduce_done():
        @pl.loop(1, n)
        def _(k):
            peer = lax.rem(t + k, n)
            if_holder(peer, lambda: rs_copy(k, peer, t, peer).wait_send())

        def sent():
            @pl.loop(0, n)
            def _(k):
                bc_copy(k, t, lax.rem(t + k, n)).wait_send()

        if_holder(t, sent)

    def receive_own():
        @pl.loop(0, n)
        def _(k):
            owner = lax.rem(t - k + n, n)

            def take():
                bc_copy(k, owner, t).wait_recv()
                for r in range(1, ndp):
                    fw_copy(r, k, d, owner).start()

            if_holder(owner, take)

    def receive_other(r):
        slot = lax.rem(d - r + ndp, ndp)

        @pl.loop(0, n)
        def _(k):
            owner = lax.rem(t - k + n, n)
            if_holder(owner, lambda: fw_copy(r, k, slot, owner).wait_recv())

    def tiles(size, tile, body):
        @pl.loop(0, size // tile)
        def _(j):
            body(pl.ds(pl.multiple_of(j * tile, tile), tile))

    def forward(x_ref, cols):
        x = x_ref[...]
        gate = dot(x, wg[:, cols]).astype(jnp.bfloat16)
        up = dot(x, wu[:, cols]).astype(jnp.bfloat16)
        return gate, up

    def first_forward(r):
        def body(cols):
            gate, up = forward(a_all.at[r], cols)
            gate_s[r, :, cols] = gate
            up_s[r, :, cols] = up
            hid[r, :, cols] = hidden_of(gate, up)

        tiles(wide, ff_tile, body)

    @pl.when(seg == 0)
    def _():
        first_forward(d)

        def down(cols):
            stage[:, cols] = dot(hid[d], wd[:, cols]).astype(jnp.bfloat16)

        tiles(depth, d_tile, down)
        reduce_rows()
        for r in range(1, ndp):
            slot = lax.rem(d - r + ndp, ndp)
            ax_copy(r, slot).wait_recv()
            first_forward(slot)
        receive_own()

        def backward(r):
            def body(cols):
                d_hidden = dot_nt(b_all[r], wd[cols, :])
                d_gate, d_up = slopes(gate_s[r, :, cols], up_s[r, :, cols], d_hidden)
                dgate[r, :, cols] = d_gate
                dup[r, :, cols] = d_up

            tiles(wide, ff_tile, body)

        backward(d)
        for r in range(1, ndp):
            receive_other(r)
            backward(lax.rem(d - r + ndp, ndp))

    @pl.when(seg == 1)
    def _():
        def early(cols):
            dhid[:, cols] = dot_nt(a_all[d], wd[cols, :])

        tiles(wide, ff_tile, early)
        receive_own()

        def turn(cols):
            gate, up = forward(b_all.at[d], cols)
            d_gate, d_up = slopes(gate, up, dhid[:, cols])
            dgate[d, :, cols] = d_gate
            dup[d, :, cols] = d_up
            hid[d, :, cols] = hidden_of(gate, up)

        tiles(wide, ff_tile, turn)

        def back(cols):
            value = dot_nt(dgate[d], wg[cols, :]) + dot_nt(dup[d], wu[cols, :])
            stage[:, cols] = value.astype(jnp.bfloat16)

        tiles(depth, d_tile, back)
        reduce_rows()
        for r in range(1, ndp):
            slot = lax.rem(d - r + ndp, ndp)
            ax_copy(r, slot).wait_recv()
            receive_other(r)

            def whole(cols):
                d_hidden = dot_nt(a_all[slot], wd[cols, :])
                gate, up = forward(b_all.at[slot], cols)
                d_gate, d_up = slopes(gate, up, d_hidden)
                dgate[slot, :, cols] = d_gate
                dup[slot, :, cols] = d_up
                hid[slot, :, cols] = hidden_of(gate, up)

            tiles(wide, ff_tile, whole)

    saves = [
        pltpu.make_async_copy(source, target, out_sem.at[i])
        for i, (source, target) in enumerate(
            ((a_all, a_out), (b_all, b_out), (hid, h_out), (dgate, dg_out), (dup, du_out))
        )
    ]
    for save in saves:
        save.start()

    @pl.loop(1, n)
    def _(k):
        ag_copy(k, t, lax.rem(t + k, n)).wait_send()

    for r in range(1, ndp):
        ax_copy(r, d).wait_send()
    reduce_done()

    @pl.loop(0, n)
    def _(k):
        owner = lax.rem(t - k + n, n)

        def forwarded():
            for r in range(1, ndp):
                fw_copy(r, k, d, owner).wait_send()

        if_holder(owner, forwarded)

    for save in saves:
        save.wait()


def grads_kernel(where, a, b, hid, dgate, dup, g_gate, g_up, g_down):
    first = where[1] == 0
    acts = jnp.where(first, a[...], b[...])
    cots = jnp.where(first, b[...], a[...])
    g_gate[0] = dot_tn(acts, dgate[...])
    g_up[0] = dot_tn(acts, dup[...])
    g_down[0] = dot_tn(hid[...], cots)


def local(n, ndp, tokens, w_gate, w_up, w_down, cotangent):
    rows, part = tokens.shape
    depth, wide = w_gate.shape[1], w_gate.shape[2]
    block = rows // n
    while block % 16:
        block *= 2
    any_spec = pl.BlockSpec(memory_space=pl.ANY)
    vmem_spec = pl.BlockSpec(memory_space=pltpu.VMEM)
    bf16, f32 = jnp.bfloat16, jnp.float32
    narrow = jax.ShapeDtypeStruct((ndp, rows, depth), bf16)
    broad = jax.ShapeDtypeStruct((ndp, rows, wide), bf16)
    dma = pltpu.SemaphoreType.DMA
    parts = pl.pallas_call(
        functools.partial(relay_kernel, n, ndp, block),
        out_shape=(narrow, narrow, broad, broad, broad),
        in_specs=[vmem_spec, vmem_spec, any_spec, any_spec, any_spec],
        out_specs=(any_spec,) * 5,
        scratch_shapes=[
            pltpu.VMEM((depth, wide), bf16),
            pltpu.VMEM((depth, wide), bf16),
            pltpu.VMEM((wide, depth), bf16),
            pltpu.VMEM((n, rows, part), bf16),
            pltpu.VMEM((ndp, rows, depth), bf16),
            pltpu.VMEM((ndp, rows, depth), bf16),
            pltpu.VMEM((ndp, rows, wide), bf16),
            pltpu.VMEM((ndp, rows, wide), bf16),
            pltpu.VMEM((ndp, rows, wide), bf16),
            pltpu.VMEM((ndp, rows, wide), bf16),
            pltpu.VMEM((ndp, rows, wide), bf16),
            pltpu.VMEM((rows, wide), f32),
            pltpu.VMEM((rows, depth), bf16),
            pltpu.VMEM((n, block, depth), bf16),
            pltpu.VMEM((block, depth), bf16),
            dma((3,)), dma((5,)), dma((n,)), dma((n,)), dma((ndp,)), dma((ndp,)),
            dma((n,)), dma((n,)), dma((n,)), dma((n,)), dma((ndp, n)), dma((ndp, n)),
        ],
        compiler_params=pltpu.CompilerParams(
            collective_id=0, has_side_effects=True, vmem_limit_bytes=VMEM_LIMIT
        ),
    )(tokens, cotangent, w_gate, w_up, w_down)
    count = ndp * rows
    a, b = (value.reshape(count, depth) for value in parts[:2])
    hid, dgate, dup = (value.reshape(count, wide) for value in parts[2:])
    share = depth // ndp
    mine = lax.axis_index("dp")
    if share % 128:
        a = lax.dynamic_slice_in_dim(a, mine * share, share, 1)
        b = lax.dynamic_slice_in_dim(b, mine * share, share, 1)
        mine = jnp.zeros_like(mine)
    where = jnp.stack([mine, lax.axis_index("segment")]).astype(jnp.int32)
    tile = 256 if wide % 256 == 0 else wide
    half = pl.BlockSpec((count, share), lambda j, where: (0, where[0]))
    strip = pl.BlockSpec((count, tile), lambda j, where: (0, j))
    tall = pl.BlockSpec((1, share, tile), lambda j, where: (0, 0, j))
    return pl.pallas_call(
        grads_kernel,
        grid_spec=pltpu.PrefetchScalarGridSpec(
            num_scalar_prefetch=1,
            grid=(wide // tile,),
            in_specs=[half, half, strip, strip, strip],
            out_specs=(tall, tall, pl.BlockSpec((1, tile, share), lambda j, where: (0, j, 0))),
        ),
        out_shape=(
            jax.ShapeDtypeStruct((1, share, wide), f32),
            jax.ShapeDtypeStruct((1, share, wide), f32),
            jax.ShapeDtypeStruct((1, wide, share), f32),
        ),
        compiler_params=pltpu.CompilerParams(vmem_limit_bytes=VMEM_LIMIT),
    )(where, a, b, hid, dgate, dup)


def solution(mesh):
    in_specs = (
        P("dp", "tensor"),
        P("segment", None, "tensor"),
        P("segment", None, "tensor"),
        P("segment", "tensor", None),
        P("dp", "tensor"),
    )
    out_specs = (
        P("segment", "dp", "tensor"),
        P("segment", "dp", "tensor"),
        P("segment", "tensor", "dp"),
    )
    run = functools.partial(local, mesh.shape["tensor"], mesh.shape["dp"])
    return jax.shard_map(run, mesh=mesh, in_specs=in_specs, out_specs=out_specs, check_vma=False)
```

time: 586 us -> 77.2 us (0.13)
  waiting for transfers between devices: 277 us -> 0 us
  blocking collectives: 187 us -> 0 us
  Pallas kernels: 0 us -> 72.5 us
  matrix products: 50.2 us -> 0 us
  starting transfers between devices: 24.5 us -> 0 us
  local copies, waits for them, and re-layouts: 18.7 us -> 3.06 us
  between operations: 14.8 us -> 0.64 us
  other arithmetic: 12.5 us -> 0.62 us
    unnamed x11 -> x0, waiting for transfers between devices: 228 us -> none
    all_gather x6 -> x0, blocking collectives: 187 us -> none  [the longest x3 94.3 us: local(): gathered = lax.all_gather(inputs, 'tensor', axis=1, tiled=True)]
    pallas_call x0 -> x2, Pallas kernels: none -> 72.5 us  [the longest x1 63.4 us: local(): pl.pallas_call(functools.partial(relay_kernel, n, ndp, block), out_shape=...]
    dot_general x18 -> x0, matrix products: 50.2 us -> none  [the longest x7 22.6 us: against_cols(): lax.dot_general(left, right, (((1,), (1,)), ((), ())), preferred_element_...]
    all_gather x3 -> x0, waiting for transfers between devices: 36.6 us -> none  [the longest x1 18.6 us: local(): lax.all_gather(all_up, 'dp', axis=0, tiled=True)]
    ppermute x12 -> x0, starting transfers between devices: 17 us -> none  [from_behind(): return lax.ppermute(block, axis, route)]
    all_to_all x2 -> x0, waiting for transfers between devices: 13 us -> none  [the longest x1 13 us: local(): lax.all_to_all(all_cot, 'dp', split_axis=1, concat_axis=0, tiled=True)]
    unnamed x37 -> x2, local copies, waits for them, and re-layouts: 15.1 us -> 3.06 us
  transfers between devices with their start and end apart: 21 -> 0, of which waited for: 8 -> 0; matrix products, arithmetic and copies ran while one was open for 11% -> 0% of each run, Pallas kernels for 0% -> 0%
where the time goes in v1:
time: 77.2 us; the launch traced here: 76.8 us
  Pallas kernels  72.5 us (94%)
  local copies, waits for them, and re-layouts  3.06 us (4%)
    pallas_call x1, Pallas kernels, local(): pl.pallas_call(functools.partial(relay_kernel, n, ndp, block), out_shape=...  63.4 us
    pallas_call x1, Pallas kernels, local(): pl.pallas_call(grads_kernel, grid_spec=pltpu.PrefetchScalarGridSpec(num_s...  9.08 us
    unnamed x2, local copies, waits for them, and re-layouts  3.06 us

profile of v1, /device:TPU:0, one launch (start us, length us, event | category | flops | bytes accessed | tf_op | source)
XLA Modules:
  0.0 76.8 jit_solution(5848105838166122873)
XLA Ops:
  0.6 0.6 pad_add_fusion.where
  1.3 1.5 %copy.8.tok = bf16[128,192]{1,0:T(8,128)(2,1)} copy(bf16[128,192]{0,1:T(8,128)(2,1)} %param.5) | data formatting | bytes 98304 | tf_op args[0]
  2.8 1.5 %copy.9.cot = bf16[128,192]{1,0:T(8,128)(2,1)} copy(bf16[128,192]{0,1:T(8,128)(2,1)} %param.9) | data formatting | bytes 98304 | tf_op args[4]
  4.3 63.4 %shard_map.76 = (bf16[2,128,1536]{2,1,0:T(8,128)(2,1)}, bf16[2,128,1536]{2,1,0:T(8,128)(2,1)}, bf16[2,128,1536]{2,1,0:T(8,128)(2,1)}, bf16[2,128,1536]{2,1,0:T(8,128)(2,1)}, bf16[2,128,1536]{2,1,0:T(8,128)(2,1)}) custom-call(bf16[128,192]{1,0:T(8,128)(2,1)} %copy.8.tok, bf16[128,192]{1,0:T(8,128)(2,1)} %copy.9.cot, bf16[1,1536,1536]{2,1,0:T(8,128)(2,1)} %wg_h.1, ...), custom_call_target="tpu_custom_call" | custom-call | tf_op jit(solution)/shard_map/pallas_call | solution.py:352
  67.7 9.1 %shard_map.77 = (f32[1,768,1536]{2,1,0:T(8,128)}, f32[1,768,1536]{2,1,0:T(8,128)}, f32[1,1536,768]{2,1,0:T(8,128)}) custom-call(s32[2]{0:T(128)} %pad_add_fusion.where, bf16[256,1536]{1,0:T(8,128)(2,1)} %bitcast.7, bf16[256,1536]{1,0:T(8,128)(2,1)} %bitcast.8, bf16[256,1536]{1,0:T(8,128)(2,1)} %bitcast.9, bf16[256,1536]{1,0:T(8,128)(2,1)} %bitcast.10, ...), custom_call_target="tpu_custom_call" | custom-call | tf_op jit(solution)/shard_map/pallas_call | solution.py:394

commit v2 on v1

--- a/solution.py
+++ b/solution.py
@@ -8,7 +8,7 @@
 from jax.sharding import PartitionSpec as P
 
 MESH = pl.DeviceIdType.MESH
-VMEM_LIMIT = 56 * 1024 * 1024
+VMEM_LIMIT = 57 * 1024 * 1024
 
 
 def tile_of(size):
@@ -25,12 +25,6 @@
 def dot_nt(left, right):
     return lax.dot_general(
         left, right, (((1,), (1,)), ((), ())), preferred_element_type=jnp.float32
-    )
-
-
-def dot_tn(left, right):
-    return lax.dot_general(
-        left, right, (((0,), (0,)), ((), ())), preferred_element_type=jnp.float32
     )
 
 
@@ -51,9 +45,9 @@
 def relay_kernel(
     n, ndp, block,
     tok, cot, wg_h, wu_h, wd_h,
-    a_out, b_out, h_out, dg_out, du_out,
+    at_out, c_out, ht_out, dg_out, du_out,
     wg, wu, wd, shards, a_all, b_all, gate_s, up_s, hid, dgate, dup, dhid, stage, sums, turned,
-    w_sem, out_sem, ag_send, ag_recv, ax_send, ax_recv, rs_send, rs_recv, bc_send, bc_recv, fw_send, fw_recv,
+    acts_t, hid_t, go, w_sem, out_sem, ag_send, ag_recv, ax_send, ax_recv, rs_send, rs_recv, bc_send, bc_recv, fw_send, fw_recv,
 ):
     seg = lax.axis_index("segment")
     t = lax.axis_index("tensor")
@@ -61,7 +55,8 @@
     other = 1 - seg
     rows, depth = a_all.shape[1], a_all.shape[2]
     wide = hid.shape[2]
-    part = tok.shape[1]
+    part = tok.shape[0]
+    share = at_out.shape[0]
     holders = rows // block
     ff_tile, d_tile = tile_of(wide), tile_of(depth)
 
@@ -90,7 +85,7 @@
         pl.semaphore_signal(
             barrier, inc=1, device_id=place(seg, t, lax.rem(d + r, ndp)), device_id_type=MESH
         )
-    shards[t] = jnp.where(seg == 0, tok[...], cot[...])
+    shards[t] = jnp.where(seg == 0, tok[...], cot[...]).T
     pl.semaphore_wait(barrier, 2 * n - 1 + ndp - 1)
 
     def ag_copy(k, slot, peer):
@@ -137,6 +132,10 @@
         else:
             pl.when(index < holders)(action)
 
+    @pl.when(seg == 1)
+    def _():
+        pl.semaphore_wait(go, 1)
+
     @pl.loop(1, n)
     def _(k):
         ag_copy(k, t, lax.rem(t + k, n)).start()
@@ -144,6 +143,10 @@
     @pl.loop(1, n)
     def _(k):
         ag_copy(k, lax.rem(t - k + n, n), t).wait_recv()
+
+    @pl.when(seg == 0)
+    def _():
+        pl.semaphore_signal(go, inc=1, device_id=place(1, t, d), device_id_type=MESH)
 
     for i in range(n):
         a_all[d, :, i * part:(i + 1) * part] = shards[i]
@@ -221,6 +224,26 @@
         up = dot(x, wu[:, cols]).astype(jnp.bfloat16)
         return gate, up
 
+    def turn_over(r, acts_ref):
+        lanes = pl.ds(pl.multiple_of(r * rows, rows), rows)
+
+        def hidden_turned(cols):
+            hid_t[cols, lanes] = hid[r, :, cols].T
+
+        def acts_turned(cols):
+            acts_t[cols, lanes] = acts_ref[r, :, cols].T
+
+        tiles(wide, ff_tile, hidden_turned)
+        tiles(depth, d_tile, acts_turned)
+
+    def save(i, cots_ref):
+        narrow = pl.ds(pl.multiple_of(d * share, share), share)
+        cots = cots_ref if c_out.shape[2] == depth else cots_ref.at[:, :, narrow]
+        source, target = (
+            (acts_t.at[narrow], at_out), (hid_t, ht_out), (cots, c_out), (dgate, dg_out), (dup, du_out)
+        )[i]
+        return pltpu.make_async_copy(source, target, out_sem.at[i])
+
     def first_forward(r):
         def body(cols):
             gate, up = forward(a_all.at[r], cols)
@@ -239,10 +262,14 @@
 
         tiles(depth, d_tile, down)
         reduce_rows()
+        turn_over(d, a_all)
         for r in range(1, ndp):
             slot = lax.rem(d - r + ndp, ndp)
             ax_copy(r, slot).wait_recv()
             first_forward(slot)
+            turn_over(slot, a_all)
+        save(0, b_all).start()
+        save(1, b_all).start()
         receive_own()
 
         def backward(r):
@@ -257,7 +284,13 @@
         backward(d)
         for r in range(1, ndp):
             receive_other(r)
+            if r == ndp - 1:
+                save(2, b_all).start()
             backward(lax.rem(d - r + ndp, ndp))
+        save(3, b_all).start()
+        save(4, b_all).start()
+        for i in range(5):
+            save(i, b_all).wait()
 
     @pl.when(seg == 1)
     def _():
@@ -282,6 +315,7 @@
 
         tiles(depth, d_tile, back)
         reduce_rows()
+        turn_over(d, b_all)
         for r in range(1, ndp):
             slot = lax.rem(d - r + ndp, ndp)
             ax_copy(r, slot).wait_recv()
@@ -296,15 +330,12 @@
                 hid[slot, :, cols] = hidden_of(gate, up)
 
             tiles(wide, ff_tile, whole)
-
-    saves = [
-        pltpu.make_async_copy(source, target, out_sem.at[i])
-        for i, (source, target) in enumerate(
-            ((a_all, a_out), (b_all, b_out), (hid, h_out), (dgate, dg_out), (dup, du_out))
-        )
-    ]
-    for save in saves:
-        save.start()
+            turn_over(slot, b_all)
+
+        for i in range(5):
+            save(i, a_all).start()
+        for i in range(5):
+            save(i, a_all).wait()
 
     @pl.loop(1, n)
     def _(k):
@@ -324,17 +355,11 @@
 
         if_holder(owner, forwarded)
 
-    for save in saves:
-        save.wait()
-
-
-def grads_kernel(where, a, b, hid, dgate, dup, g_gate, g_up, g_down):
-    first = where[1] == 0
-    acts = jnp.where(first, a[...], b[...])
-    cots = jnp.where(first, b[...], a[...])
-    g_gate[0] = dot_tn(acts, dgate[...])
-    g_up[0] = dot_tn(acts, dup[...])
-    g_down[0] = dot_tn(hid[...], cots)
+
+def grads_kernel(acts_t, hid_t, cots, dgate, dup, g_gate, g_up, g_down):
+    g_gate[0] = dot(acts_t[...], dgate[...])
+    g_up[0] = dot(acts_t[...], dup[...])
+    g_down[0] = dot(hid_t[...], cots[...])
 
 
 def local(n, ndp, tokens, w_gate, w_up, w_down, cotangent):
@@ -344,15 +369,23 @@
     while block % 16:
         block *= 2
     any_spec = pl.BlockSpec(memory_space=pl.ANY)
+    hbm_spec = pl.BlockSpec(memory_space=pltpu.HBM)
     vmem_spec = pl.BlockSpec(memory_space=pltpu.VMEM)
     bf16, f32 = jnp.bfloat16, jnp.float32
-    narrow = jax.ShapeDtypeStruct((ndp, rows, depth), bf16)
+    share, count = depth // ndp, ndp * rows
+    kept = depth if share % 128 else share
     broad = jax.ShapeDtypeStruct((ndp, rows, wide), bf16)
     dma = pltpu.SemaphoreType.DMA
     parts = pl.pallas_call(
         functools.partial(relay_kernel, n, ndp, block),
-        out_shape=(narrow, narrow, broad, broad, broad),
-        in_specs=[vmem_spec, vmem_spec, any_spec, any_spec, any_spec],
+        out_shape=(
+            jax.ShapeDtypeStruct((share, count), bf16),
+            jax.ShapeDtypeStruct((ndp, rows, kept), bf16),
+            jax.ShapeDtypeStruct((wide, count), bf16),
+            broad,
+            broad,
+        ),
+        in_specs=[vmem_spec, vmem_spec, hbm_spec, hbm_spec, hbm_spec],
         out_specs=(any_spec,) * 5,
         scratch_shapes=[
             pltpu.VMEM((depth, wide), bf16),
@@ -370,42 +403,42 @@
             pltpu.VMEM((rows, depth), bf16),
             pltpu.VMEM((n, block, depth), bf16),
             pltpu.VMEM((block, depth), bf16),
+            pltpu.VMEM((depth, count), bf16),
+            pltpu.VMEM((wide, count), bf16),
+            pltpu.SemaphoreType.REGULAR,
             dma((3,)), dma((5,)), dma((n,)), dma((n,)), dma((ndp,)), dma((ndp,)),
             dma((n,)), dma((n,)), dma((n,)), dma((n,)), dma((ndp, n)), dma((ndp, n)),
         ],
         compiler_params=pltpu.CompilerParams(
             collective_id=0, has_side_effects=True, vmem_limit_bytes=VMEM_LIMIT
         ),
-    )(tokens, cotangent, w_gate, w_up, w_down)
-    count = ndp * rows
-    a, b = (value.reshape(count, depth) for value in parts[:2])
-    hid, dgate, dup = (value.reshape(count, wide) for value in parts[2:])
-    share = depth // ndp
-    mine = lax.axis_index("dp")
-    if share % 128:
-        a = lax.dynamic_slice_in_dim(a, mine * share, share, 1)
-        b = lax.dynamic_slice_in_dim(b, mine * share, share, 1)
-        mine = jnp.zeros_like(mine)
-    where = jnp.stack([mine, lax.axis_index("segment")]).astype(jnp.int32)
+    )(tokens.T, cotangent.T, w_gate, w_up, w_down)
+    acts_t, cots, hid_t, dgate, dup = parts
+    if kept != share:
+        cots = lax.dynamic_slice_in_dim(cots, lax.axis_index("dp") * share, share, 2)
+    cots = cots.reshape(count, share)
+    dgate, dup = (value.reshape(count, wide) for value in (dgate, dup))
     tile = 256 if wide % 256 == 0 else wide
-    half = pl.BlockSpec((count, share), lambda j, where: (0, where[0]))
-    strip = pl.BlockSpec((count, tile), lambda j, where: (0, j))
-    tall = pl.BlockSpec((1, share, tile), lambda j, where: (0, 0, j))
+    strip = pl.BlockSpec((count, tile), lambda j: (0, j))
+    tall = pl.BlockSpec((1, share, tile), lambda j: (0, 0, j))
     return pl.pallas_call(
         grads_kernel,
-        grid_spec=pltpu.PrefetchScalarGridSpec(
-            num_scalar_prefetch=1,
-            grid=(wide // tile,),
-            in_specs=[half, half, strip, strip, strip],
-            out_specs=(tall, tall, pl.BlockSpec((1, tile, share), lambda j, where: (0, j, 0))),
-        ),
+        grid=(wide // tile,),
+        in_specs=[
+            pl.BlockSpec((share, count), lambda j: (0, 0)),
+            pl.BlockSpec((tile, count), lambda j: (j, 0)),
+            pl.BlockSpec((count, share), lambda j: (0, 0)),
+            strip,
+            strip,
+        ],
+        out_specs=(tall, tall, pl.BlockSpec((1, tile, share), lambda j: (0, j, 0))),
         out_shape=(
             jax.ShapeDtypeStruct((1, share, wide), f32),
             jax.ShapeDtypeStruct((1, share, wide), f32),
             jax.ShapeDtypeStruct((1, wide, share), f32),
         ),
         compiler_params=pltpu.CompilerParams(vmem_limit_bytes=VMEM_LIMIT),
-    )(where, a, b, hid, dgate, dup)
+    )(acts_t, hid_t, cots, dgate, dup)
 
 
 def solution(mesh):

time: 77.2 us -> 68.4 us (0.89)
  Pallas kernels: 72.5 us -> 67.5 us
  local copies, waits for them, and re-layouts: 3.06 us -> 0 us
    pallas_call x1, Pallas kernels: 63.4 us -> 59.2 us  [local(): pl.pallas_call(functools.partial(relay_kernel, n, ndp, block), out_shape=...]
    unnamed x2 -> x0, local copies, waits for them, and re-layouts: 3.06 us -> none
    pallas_call x1, Pallas kernels: 9.08 us -> 8.28 us  [local(): pl.pallas_call(grads_kernel, grid=(wide // tile,), in_specs=[pl.BlockSpec...]
where the time goes in v2:
time: 68.4 us; the launch traced here: 68.1 us
  Pallas kernels  67.5 us (99%)
    pallas_call x1, Pallas kernels, local(): pl.pallas_call(functools.partial(relay_kernel, n, ndp, block), out_shape=...  59.2 us
    pallas_call x1, Pallas kernels, local(): pl.pallas_call(grads_kernel, grid=(wide // tile,), in_specs=[pl.BlockSpec...  8.28 us

profile of v2, /device:TPU:0, one launch (start us, length us, event | category | flops | bytes accessed | tf_op | source)
XLA Modules:
  0.0 68.1 jit_solution(17320436399055716355)
XLA Ops:
  0.6 59.2 %shard_map.76 = (bf16[768,256]{1,0:T(8,128)(2,1)}, bf16[2,128,768]{2,1,0:T(8,128)(2,1)}, bf16[1536,256]{1,0:T(8,128)(2,1)}, bf16[2,128,1536]{2,1,0:T(8,128)(2,1)}, bf16[2,128,1536]{2,1,0:T(8,128)(2,1)}) custom-call(bf16[192,128]{1,0:T(8,128)(2,1)} %bitcast.8, bf16[192,128]{1,0:T(8,128)(2,1)} %bitcast.9, bf16[1,1536,1536]{2,1,0:T(8,128)(2,1)} %wg_h.1, ...), custom_call_target="tpu_custom_call" | custom-call | tf_op jit(solution)/shard_map/pallas_call | solution.py:379
  59.8 8.3 %shard_map.77 = (f32[1,768,1536]{2,1,0:T(8,128)}, f32[1,768,1536]{2,1,0:T(8,128)}, f32[1,1536,768]{2,1,0:T(8,128)}) custom-call(bf16[768,256]{1,0:T(8,128)(2,1)} %get-tuple-element.8.acts_t, bf16[1536,256]{1,0:T(8,128)(2,1)} %get-tuple-element.9.hid_t, bf16[256,768]{1,0:T(8,128)(2,1)} %bitcast.7, bf16[256,1536]{1,0:T(8,128)(2,1)} %bitcast.5, ...), custom_call_target="tpu_custom_call" | custom-call | tf_op jit(solution)/shard_map/pallas_call | solution.py:424

commit v3 on v2

--- a/solution.py
+++ b/solution.py
@@ -102,19 +102,22 @@
             device_id=place(seg, t, lax.rem(d + r, ndp)), device_id_type=MESH,
         )
 
-    def rs_copy(k, owner, slot, peer):
+    def columns(c):
+        return pl.ds(pl.multiple_of(c * d_tile, d_tile), d_tile)
+
+    def rs_copy(k, c, owner, slot, peer):
         return pltpu.make_async_remote_copy(
-            src_ref=stage.at[pl.ds(pl.multiple_of(owner * block, block), block)],
-            dst_ref=sums.at[slot],
-            send_sem=rs_send.at[k], recv_sem=rs_recv.at[k],
+            src_ref=stage.at[pl.ds(pl.multiple_of(owner * block, block), block), columns(c)],
+            dst_ref=sums.at[slot, :, columns(c)],
+            send_sem=rs_send.at[k, c], recv_sem=rs_recv.at[k, c],
             device_id=place(seg, peer, d), device_id_type=MESH,
         )
 
-    def bc_copy(k, owner, peer):
+    def bc_copy(k, c, owner, peer):
         return pltpu.make_async_remote_copy(
-            src_ref=turned,
-            dst_ref=b_all.at[d, pl.ds(pl.multiple_of(owner * block, block), block)],
-            send_sem=bc_send.at[k], recv_sem=bc_recv.at[k],
+            src_ref=turned.at[:, columns(c)],
+            dst_ref=b_all.at[d, pl.ds(pl.multiple_of(owner * block, block), block), columns(c)],
+            send_sem=bc_send.at[k, c], recv_sem=bc_recv.at[k, c],
             device_id=place(other, peer, d), device_id_type=MESH,
         )
 
@@ -155,41 +158,55 @@
     for load in loads:
         load.wait()
 
-    def reduce_rows():
-        @pl.loop(1, n)
-        def _(k):
-            peer = lax.rem(t + k, n)
-            if_holder(peer, lambda: rs_copy(k, peer, t, peer).start())
+    chunks = depth // d_tile
+
+    def reduce_rows(product):
+        @pl.loop(0, chunks)
+        def _(c):
+            stage[:, columns(c)] = product(columns(c)).astype(jnp.bfloat16)
+
+            @pl.loop(1, n)
+            def _(k):
+                peer = lax.rem(t + k, n)
+                if_holder(peer, lambda: rs_copy(k, c, peer, t, peer).start())
 
         def total():
             mine = pl.ds(pl.multiple_of(t * block, block), block)
             sums[t] = stage[mine, :]
 
+            @pl.loop(0, chunks)
+            def _(c):
+                @pl.loop(1, n)
+                def _(k):
+                    rs_copy(k, c, t, lax.rem(t - k + n, n), t).wait_recv()
+
+                cols = columns(c)
+                value = sums[0, :, cols].astype(jnp.float32)
+                for i in range(1, n):
+                    value = value + sums[i, :, cols].astype(jnp.float32)
+                value = a_all[d, mine, cols].astype(jnp.float32) + value
+                turned[:, cols] = value.astype(jnp.bfloat16)
+
+                @pl.loop(0, n)
+                def _(k):
+                    bc_copy(k, c, t, lax.rem(t + k, n)).start()
+
+        if_holder(t, total)
+
+    def reduce_done():
+        @pl.loop(0, chunks)
+        def _(c):
             @pl.loop(1, n)
             def _(k):
-                rs_copy(k, t, lax.rem(t - k + n, n), t).wait_recv()
-
-            value = sums[0].astype(jnp.float32)
-            for i in range(1, n):
-                value = value + sums[i].astype(jnp.float32)
-            turned[...] = (a_all[d, mine, :].astype(jnp.float32) + value).astype(jnp.bfloat16)
-
-            @pl.loop(0, n)
-            def _(k):
-                bc_copy(k, t, lax.rem(t + k, n)).start()
-
-        if_holder(t, total)
-
-    def reduce_done():
-        @pl.loop(1, n)
-        def _(k):
-            peer = lax.rem(t + k, n)
-            if_holder(peer, lambda: rs_copy(k, peer, t, peer).wait_send())
+                peer = lax.rem(t + k, n)
+                if_holder(peer, lambda: rs_copy(k, c, peer, t, peer).wait_send())
 
         def sent():
-            @pl.loop(0, n)
-            def _(k):
-                bc_copy(k, t, lax.rem(t + k, n)).wait_send()
+            @pl.loop(0, chunks)
+            def _(c):
+                @pl.loop(0, n)
+                def _(k):
+                    bc_copy(k, c, t, lax.rem(t + k, n)).wait_send()
 
         if_holder(t, sent)
 
@@ -199,7 +216,10 @@
             owner = lax.rem(t - k + n, n)
 
             def take():
-                bc_copy(k, owner, t).wait_recv()
+                @pl.loop(0, chunks)
+                def _(c):
+                    bc_copy(k, c, owner, t).wait_recv()
+
                 for r in range(1, ndp):
                     fw_copy(r, k, d, owner).start()
 
@@ -257,11 +277,7 @@
     def _():
         first_forward(d)
 
-        def down(cols):
-            stage[:, cols] = dot(hid[d], wd[:, cols]).astype(jnp.bfloat16)
-
-        tiles(depth, d_tile, down)
-        reduce_rows()
+        reduce_rows(lambda cols: dot(hid[d], wd[:, cols]))
         turn_over(d, a_all)
         for r in range(1, ndp):
             slot = lax.rem(d - r + ndp, ndp)
@@ -309,12 +325,7 @@
 
         tiles(wide, ff_tile, turn)
 
-        def back(cols):
-            value = dot_nt(dgate[d], wg[cols, :]) + dot_nt(dup[d], wu[cols, :])
-            stage[:, cols] = value.astype(jnp.bfloat16)
-
-        tiles(depth, d_tile, back)
-        reduce_rows()
+        reduce_rows(lambda cols: dot_nt(dgate[d], wg[cols, :]) + dot_nt(dup[d], wu[cols, :]))
         turn_over(d, b_all)
         for r in range(1, ndp):
             slot = lax.rem(d - r + ndp, ndp)
@@ -376,6 +387,7 @@
     kept = depth if share % 128 else share
     broad = jax.ShapeDtypeStruct((ndp, rows, wide), bf16)
     dma = pltpu.SemaphoreType.DMA
+    chunks = depth // tile_of(depth)
     parts = pl.pallas_call(
         functools.partial(relay_kernel, n, ndp, block),
         out_shape=(
@@ -407,7 +419,7 @@
             pltpu.VMEM((wide, count), bf16),
             pltpu.SemaphoreType.REGULAR,
             dma((3,)), dma((5,)), dma((n,)), dma((n,)), dma((ndp,)), dma((ndp,)),
-            dma((n,)), dma((n,)), dma((n,)), dma((n,)), dma((ndp, n)), dma((ndp, n)),
+            dma((n, chunks)), dma((n, chunks)), dma((n, chunks)), dma((n, chunks)), dma((ndp, n)), dma((ndp, n)),
         ],
         compiler_params=pltpu.CompilerParams(
             collective_id=0, has_side_effects=True, vmem_limit_bytes=VMEM_LIMIT
@@ -418,7 +430,7 @@
         cots = lax.dynamic_slice_in_dim(cots, lax.axis_index("dp") * share, share, 2)
     cots = cots.reshape(count, share)
     dgate, dup = (value.reshape(count, wide) for value in (dgate, dup))
-    tile = 256 if wide % 256 == 0 else wide
+    tile = tile_of(wide)
     strip = pl.BlockSpec((count, tile), lambda j: (0, j))
     tall = pl.BlockSpec((1, share, tile), lambda j: (0, 0, j))
     return pl.pallas_call(

time: 68.4 us -> 65.5 us (0.958)
  Pallas kernels: 67.5 us -> 64.6 us
    pallas_call x1, Pallas kernels: 59.2 us -> 57.5 us  [local(): pl.pallas_call(functools.partial(relay_kernel, n, ndp, block), out_shape=...]
    pallas_call x1, Pallas kernels: 8.28 us -> 7.17 us  [local(): pl.pallas_call(grads_kernel, grid=(wide // tile,), in_specs=[pl.BlockSpec...]
where the time goes in v3:
time: 65.5 us; the launch traced here: 65.3 us
  Pallas kernels  64.6 us (99%)
    pallas_call x1, Pallas kernels, local(): pl.pallas_call(functools.partial(relay_kernel, n, ndp, block), out_shape=...  57.5 us
    pallas_call x1, Pallas kernels, local(): pl.pallas_call(grads_kernel, grid=(wide // tile,), in_specs=[pl.BlockSpec...  7.17 us

profile of v3, /device:TPU:0, one launch (start us, length us, event | category | flops | bytes accessed | tf_op | source)
XLA Modules:
  0.0 65.3 jit_solution(10470109213971932580)
XLA Ops:
  0.6 57.5 %shard_map.76 = (bf16[768,256]{1,0:T(8,128)(2,1)}, bf16[2,128,768]{2,1,0:T(8,128)(2,1)}, bf16[1536,256]{1,0:T(8,128)(2,1)}, bf16[2,128,1536]{2,1,0:T(8,128)(2,1)}, bf16[2,128,1536]{2,1,0:T(8,128)(2,1)}) custom-call(bf16[192,128]{1,0:T(8,128)(2,1)} %bitcast.8, bf16[192,128]{1,0:T(8,128)(2,1)} %bitcast.9, bf16[1,1536,1536]{2,1,0:T(8,128)(2,1)} %wg_h.1, ...), custom_call_target="tpu_custom_call" | custom-call | tf_op jit(solution)/shard_map/pallas_call | solution.py:391
  58.1 7.2 %shard_map.77 = (f32[1,768,1536]{2,1,0:T(8,128)}, f32[1,768,1536]{2,1,0:T(8,128)}, f32[1,1536,768]{2,1,0:T(8,128)}) custom-call(bf16[768,256]{1,0:T(8,128)(2,1)} %get-tuple-element.8.acts_t, bf16[1536,256]{1,0:T(8,128)(2,1)} %get-tuple-element.9.hid_t, bf16[256,768]{1,0:T(8,128)(2,1)} %bitcast.7, bf16[256,1536]{1,0:T(8,128)(2,1)} %bitcast.5, ...), custom_call_target="tpu_custom_call" | custom-call | tf_op jit(solution)/shard_map/pallas_call | solution.py:436

commit v4 on v3

--- a/solution.py
+++ b/solution.py
@@ -139,7 +139,7 @@
     def _():
         pl.semaphore_wait(go, 1)
 
-    @pl.loop(1, n)
+    @pl.loop(1, n, unroll=True)
     def _(k):
         ag_copy(k, t, lax.rem(t + k, n)).start()
 
@@ -187,7 +187,7 @@
                 value = a_all[d, mine, cols].astype(jnp.float32) + value
                 turned[:, cols] = value.astype(jnp.bfloat16)
 
-                @pl.loop(0, n)
+                @pl.loop(0, n, unroll=True)
                 def _(k):
                     bc_copy(k, c, t, lax.rem(t + k, n)).start()
 
@@ -272,6 +272,26 @@
             hid[r, :, cols] = hidden_of(gate, up)
 
         tiles(wide, ff_tile, body)
+
+    def early_sent():
+        @pl.loop(1, n)
+        def _(k):
+            ag_copy(k, t, lax.rem(t + k, n)).wait_send()
+
+        for r in range(1, ndp):
+            ax_copy(r, d).wait_send()
+        reduce_done()
+
+    def forwards_sent():
+        @pl.loop(0, n)
+        def _(k):
+            owner = lax.rem(t - k + n, n)
+
+            def forwarded():
+                for r in range(1, ndp):
+                    fw_copy(r, k, d, owner).wait_send()
+
+            if_holder(owner, forwarded)
 
     @pl.when(seg == 0)
     def _():
@@ -286,6 +306,7 @@
             turn_over(slot, a_all)
         save(0, b_all).start()
         save(1, b_all).start()
+        early_sent()
         receive_own()
 
         def backward(r):
@@ -305,6 +326,7 @@
             backward(lax.rem(d - r + ndp, ndp))
         save(3, b_all).start()
         save(4, b_all).start()
+        forwards_sent()
         for i in range(5):
             save(i, b_all).wait()
 
@@ -345,26 +367,10 @@
 
         for i in range(5):
             save(i, a_all).start()
+        early_sent()
+        forwards_sent()
         for i in range(5):
             save(i, a_all).wait()
-
-    @pl.loop(1, n)
-    def _(k):
-        ag_copy(k, t, lax.rem(t + k, n)).wait_send()
-
-    for r in range(1, ndp):
-        ax_copy(r, d).wait_send()
-    reduce_done()
-
-    @pl.loop(0, n)
-    def _(k):
-        owner = lax.rem(t - k + n, n)
-
-        def forwarded():
-            for r in range(1, ndp):
-                fw_copy(r, k, d, owner).wait_send()
-
-        if_holder(owner, forwarded)
 
 
 def grads_kernel(acts_t, hid_t, cots, dgate, dup, g_gate, g_up, g_down):

time: 65.5 us -> 65.7 us (level)
  no operation moved by 1% of the time
where the time goes in v4:
time: 65.7 us; the launch traced here: 65.5 us
  Pallas kernels  64.9 us (99%)
    pallas_call x1, Pallas kernels, local(): pl.pallas_call(functools.partial(relay_kernel, n, ndp, block), out_shape=...  57.7 us
    pallas_call x1, Pallas kernels, local(): pl.pallas_call(grads_kernel, grid=(wide // tile,), in_specs=[pl.BlockSpec...  7.17 us

profile of v4, /device:TPU:0, one launch (start us, length us, event | category | flops | bytes accessed | tf_op | source)
XLA Modules:
  0.0 65.5 jit_solution(4056978461506204946)
XLA Ops:
  0.6 57.7 %shard_map.76 = (bf16[768,256]{1,0:T(8,128)(2,1)}, bf16[2,128,768]{2,1,0:T(8,128)(2,1)}, bf16[1536,256]{1,0:T(8,128)(2,1)}, bf16[2,128,1536]{2,1,0:T(8,128)(2,1)}, bf16[2,128,1536]{2,1,0:T(8,128)(2,1)}) custom-call(bf16[192,128]{1,0:T(8,128)(2,1)} %bitcast.8, bf16[192,128]{1,0:T(8,128)(2,1)} %bitcast.9, bf16[1,1536,1536]{2,1,0:T(8,128)(2,1)} %wg_h.1, ...), custom_call_target="tpu_custom_call" | custom-call | tf_op jit(solution)/shard_map/pallas_call | solution.py:397
  58.4 7.2 %shard_map.77 = (f32[1,768,1536]{2,1,0:T(8,128)}, f32[1,768,1536]{2,1,0:T(8,128)}, f32[1,1536,768]{2,1,0:T(8,128)}) custom-call(bf16[768,256]{1,0:T(8,128)(2,1)} %get-tuple-element.8.acts_t, bf16[1536,256]{1,0:T(8,128)(2,1)} %get-tuple-element.9.hid_t, bf16[256,768]{1,0:T(8,128)(2,1)} %bitcast.7, bf16[256,1536]{1,0:T(8,128)(2,1)} %bitcast.5, ...), custom_call_target="tpu_custom_call" | custom-call | tf_op jit(solution)/shard_map/pallas_call | solution.py:442
